TPU v7x, 32 devices: a whole 2x2x4 slice. The times are simulated.
32 devices in a mesh: section: 2 (over x), expert: 4 (over z), tensor: 4 (over y, core).
Axes of the slice: x: 2, y: 2, z: 4, core: 2. Of those that a mesh axis runs over, the one named last changes fastest.
Arguments:
- tokens: bfloat16 [64, 6144], P(('section', 'expert'), 'tensor'), may hold values from -6 to 6
- routes: int32 [64, 2], P(('section', 'expert')), may hold values from 0 to 3, all different within a row; in each aligned block of 8 rows (0 to 7, 8 to 15, ...) at most 8 rows name the same one
- router: float32 [6144, 4], replicated, may hold values from -0.18 to 0.18
- gate_proj: bfloat16 [4, 6144, 8192], P('expert', None, ('section', 'tensor')), may hold values from -0.078125 to 0.078125
- up_proj: bfloat16 [4, 6144, 8192], P('expert', None, ('section', 'tensor')), may hold values from -0.078125 to 0.078125
- down_proj: bfloat16 [4, 8192, 6144], P('expert', ('section', 'tensor')), may hold values from -0.09375 to 0.09375
- grad_out: bfloat16 [64, 6144], P(('section', 'expert'), 'tensor'), may hold values from -6 to 6
Outputs:
- moe_out: bfloat16 [64, 6144], P(('section', 'expert'), 'tensor')
- grad_tokens: bfloat16 [64, 6144], P(('section', 'expert'), 'tensor')
- grad_router: float32 [6144, 4], P('tensor')
Inputs may be any that keep to these rules, and one draw needn't show every extreme that they name: `routes`: each token names 2 different experts; in each aligned block of 8 tokens (the tokens of one group) no expert is named by more than 8 tokens, and in some blocks one expert is named by exactly 8.
All inputs are finite; a program needn't handle non-finite values.
Results may differ from a plain program's by a relative error of at most 0.02.
Values may be sent and summed in bfloat16 or wider, within the bound.
A program may use at most 128 MiB of HBM per device.

v0:
```python
import jax
import jax.numpy as jnp
from jax import lax
from jax.sharding import PartitionSpec as P

precise = lax.Precision.HIGHEST


def route_table(routes, expert_count, capacity):
    flat_ids = routes.reshape(-1)
    expert_hot = (flat_ids[:, None] == jnp.arange(expert_count, dtype=jnp.int32)[None, :]).astype(
        jnp.float32
    )
    earlier = jnp.cumsum(expert_hot, axis=0) - expert_hot
    slot_ids = jnp.sum(earlier * expert_hot, axis=1).astype(jnp.int32)
    slot_hot = (slot_ids[:, None] == jnp.arange(capacity, dtype=jnp.int32)[None, :]).astype(
        jnp.float32
    )
    routing = expert_hot.T[:, None, :] * slot_hot.T[None, :, :]
    return routing.reshape(expert_count * capacity, flat_ids.shape[0])


def gate_weights(logits, routes):
    chosen = jnp.take_along_axis(logits, routes, axis=1)
    scores = jax.nn.sigmoid(chosen)
    totals = jnp.sum(scores, axis=1, keepdims=True)
    return (scores, scores / totals)


def expert_front(rows_x, gate_mat, up_mat):
    pre_gate = jnp.dot(rows_x, gate_mat, preferred_element_type=jnp.float32)
    pre_up = jnp.dot(rows_x, up_mat, preferred_element_type=jnp.float32)
    gate_sig = jax.nn.sigmoid(pre_gate)
    gate_act = pre_gate * gate_sig
    hidden = (gate_act * pre_up).astype(jnp.bfloat16)
    return (pre_gate, pre_up, gate_sig, gate_act, hidden)


def expert_grads(grad_hidden, pre_gate, pre_up, gate_sig, gate_act):
    grad_gate = (grad_hidden * pre_up * gate_sig * (1.0 + pre_gate * (1.0 - gate_sig))).astype(
        jnp.bfloat16
    )
    grad_up = (grad_hidden * gate_act).astype(jnp.bfloat16)
    return (grad_gate, grad_up)


def router_grads(grad_weight, scores, routes, expert_count):
    totals = scores[:, 0] + scores[:, 1]
    first = (grad_weight[:, 0] - grad_weight[:, 1]) * scores[:, 1] / (totals * totals)
    second = (grad_weight[:, 1] - grad_weight[:, 0]) * scores[:, 0] / (totals * totals)
    grad_scores = jnp.stack([first, second], axis=1)
    grad_chosen = grad_scores * scores * (1.0 - scores)
    expert_hot = (
        routes[:, :, None] == jnp.arange(expert_count, dtype=jnp.int32)[None, None, :]
    ).astype(jnp.float32)
    return jnp.sum(expert_hot * grad_chosen[:, :, None], axis=1)


def contract_last(left, right):
    return lax.dot_general(
        left, right, (((1,), (1,)), ((), ())), preferred_element_type=jnp.float32
    )


def on_device(tokens, routes, router, gate_proj, up_proj, down_proj, grad_out):
    tok_rows, quarter = tokens.shape
    tensor_count = lax.axis_size("tensor")
    expert_count = lax.axis_size("expert")
    top_count = routes.shape[1]
    capacity = 2 * tok_rows * top_count // expert_count
    block_rows = expert_count * capacity
    tensor_index = lax.axis_index("tensor")
    router_rows = lax.dynamic_slice_in_dim(router, tensor_index * quarter, quarter, 0)
    routing = route_table(routes, expert_count, capacity)
    gate_mat = gate_proj[0]
    up_mat = up_proj[0]
    down_mat = down_proj[0]
    send_x, send_dy = (tokens, grad_out)
    logits = lax.psum(jnp.dot(tokens.astype(jnp.float32), router_rows, precision=precise), "tensor")
    scores, weight = gate_weights(logits, routes)
    row_width = send_x.shape[1]
    x_sent = jnp.dot(
        routing, jnp.repeat(send_x.astype(jnp.float32), top_count, axis=0), precision=precise
    )
    x_sent = x_sent.astype(jnp.bfloat16).reshape(expert_count, capacity, row_width)
    scaled = jnp.repeat(send_dy.astype(jnp.float32), top_count, axis=0) * weight.reshape(-1, 1)
    dy_sent = (
        jnp.dot(routing, scaled, precision=precise)
        .astype(jnp.bfloat16)
        .reshape(expert_count, capacity, row_width)
    )

    def block_ids(count):
        return jnp.arange(count // block_rows, dtype=jnp.int32)

    def forward_block(hidden, block):
        section_at = block // tensor_count
        tensor_at = block % tensor_count
        hidden_rows = lax.dynamic_slice_in_dim(hidden, section_at * block_rows, block_rows, 0)
        columns = lax.dynamic_slice_in_dim(down_mat, tensor_at * quarter, quarter, 1)
        return jnp.dot(hidden_rows, columns, preferred_element_type=jnp.float32)

    def backward_block(grad_gate, grad_up, block):
        section_at = block // tensor_count
        tensor_at = block % tensor_count
        gate_rows = lax.dynamic_slice_in_dim(grad_gate, section_at * block_rows, block_rows, 0)
        up_rows = lax.dynamic_slice_in_dim(grad_up, section_at * block_rows, block_rows, 0)
        gate_part = lax.dynamic_slice_in_dim(gate_mat, tensor_at * quarter, quarter, 0)
        up_part = lax.dynamic_slice_in_dim(up_mat, tensor_at * quarter, quarter, 0)
        return contract_last(gate_rows, gate_part) + contract_last(up_rows, up_part)

    landed_x = lax.all_to_all(x_sent, "expert", split_axis=0, concat_axis=0, tiled=True)
    landed_x = lax.all_gather(landed_x, "tensor", axis=2, tiled=True)
    rows_x = lax.all_gather(landed_x.reshape(block_rows, -1), "section", axis=0, tiled=True)
    pre_gate, pre_up, gate_sig, gate_act, hidden = expert_front(rows_x, gate_mat, up_mat)
    summed_out = lax.psum_scatter(
        lax.map(
            lambda block: forward_block(hidden, block),
            block_ids(lax.axis_size(("section", "tensor")) * block_rows),
        )
        .reshape(lax.axis_size(("section", "tensor")) * block_rows, quarter)
        .astype(jnp.bfloat16),
        ("section", "tensor"),
        scatter_dimension=0,
        tiled=True,
    ).astype(jnp.float32)
    expert_out = lax.all_to_all(
        summed_out.reshape(expert_count, capacity, quarter).astype(jnp.bfloat16),
        "expert",
        split_axis=0,
        concat_axis=0,
        tiled=True,
    ).astype(jnp.float32)
    landed_dy = lax.all_to_all(dy_sent, "expert", split_axis=0, concat_axis=0, tiled=True)
    landed_dy = lax.all_gather(landed_dy, "tensor", axis=2, tiled=True)
    rows_dy = lax.all_gather(landed_dy.reshape(block_rows, -1), "section", axis=0, tiled=True)
    grad_hidden = contract_last(rows_dy, down_mat)
    grad_gate, grad_up = expert_grads(grad_hidden, pre_gate, pre_up, gate_sig, gate_act)
    summed_grad = lax.psum_scatter(
        lax.map(
            lambda block: backward_block(grad_gate, grad_up, block),
            block_ids(lax.axis_size(("section", "tensor")) * block_rows),
        )
        .reshape(lax.axis_size(("section", "tensor")) * block_rows, quarter)
        .astype(jnp.bfloat16),
        ("section", "tensor"),
        scatter_dimension=0,
        tiled=True,
    ).astype(jnp.float32)
    expert_grad = lax.all_to_all(
        summed_grad.reshape(expert_count, capacity, quarter).astype(jnp.bfloat16),
        "expert",
        split_axis=0,
        concat_axis=0,
        tiled=True,
    ).astype(jnp.float32)
    out_route = jnp.dot(
        routing.T, expert_out.reshape(block_rows, quarter), precision=precise
    ).reshape(tok_rows, top_count, quarter)
    grad_route = jnp.dot(
        routing.T, expert_grad.reshape(block_rows, quarter), precision=precise
    ).reshape(tok_rows, top_count, quarter)
    moe_out = jnp.sum(weight[:, :, None] * out_route, axis=1).astype(jnp.bfloat16)
    weight_part = jnp.sum(grad_out.astype(jnp.float32)[:, None, :] * out_route, axis=2)
    grad_weight = lax.psum(weight_part, "tensor")
    grad_logits = router_grads(grad_weight, scores, routes, expert_count)
    grad_tokens = (
        jnp.sum(grad_route, axis=1) + jnp.dot(grad_logits, router_rows.T, precision=precise)
    ).astype(jnp.bfloat16)
    router_part = jnp.dot(tokens.astype(jnp.float32).T, grad_logits, precision=precise)
    grad_router = lax.psum(router_part, ("section", "expert"))
    return (moe_out, grad_tokens, grad_router)


def solution(mesh):
    return jax.shard_map(
        on_device,
        mesh=mesh,
        in_specs=(
            P(("section", "expert"), "tensor"),
            P(("section", "expert"), None),
            P(),
            P("expert", None, ("section", "tensor")),
            P("expert", None, ("section", "tensor")),
            P("expert", ("section", "tensor"), None),
            P(("section", "expert"), "tensor"),
        ),
        out_specs=(
            P(("section", "expert"), "tensor"),
            P(("section", "expert"), "tensor"),
            P("tensor", None),
        ),
        check_vma=False,
    )
```

profile of v0, /device:TPU:0, one launch (start us, length us, event | category | flops | bytes accessed | tf_op | source)
XLA Modules:
  0.0 306.5 jit_solution(3362692333737877200)
XLA Ops:
  7.2 0.8 copy.52
  9.2 0.9 fusion.27
  10.1 6.3 %all-to-all-start = ((bf16[4,8,1536]{2,1,0:T(8,128)(2,1)}), bf16[4,8,1536]{2,1,0:T(8,128)(2,1)S(1)}, u32[]{:S(2)}, u32[]{:S(2)}) async-start(bf16[4,8,1536]{2,1,0:T(8,128)(2,1)} %fusion.27), calls=%async_computation | async-start | bytes 196608 | tf_op jit(solution)/shard_map/all_to_all | solution.py:112
  17.2 0.9 convolution_bitcast_fusion.1
  18.0 6.6 %psum.21 = f32[8,4]{0,1:T(4,128)S(1)} all-reduce(f32[8,4]{0,1:T(4,128)S(1)} %convolution_bitcast_fusion.1), channel_id=1, replica_groups=mesh['section'=2,'expert'=4,'tensor'=4] {'tensor'}, use_global_device_ids=true, to_apply=%region_0.0 | all-reduce | flops 32 | bytes 256 | tf_op jit(solution)/shard_map/psum | solution.py:79
  27.4 0.9 fusion.28
  28.3 4.5 %all-to-all-start.2 = ((bf16[4,8,1536]{2,1,0:T(8,128)(2,1)}), bf16[4,8,1536]{2,1,0:T(8,128)(2,1)S(1)}, u32[]{:S(2)}, u32[]{:S(2)}) async-start(bf16[4,8,1536]{2,1,0:T(8,128)(2,1)} %fusion.28), calls=%async_computation.3 | async-start | bytes 196608 | tf_op jit(solution)/shard_map/all_to_all | solution.py:134
  32.9 6.3 %all_gather.12 = bf16[4,8,6144]{2,1,0:T(8,128)(2,1)S(1)} all-gather(bf16[4,8,1536]{2,1,0:T(8,128)(2,1)S(1)} %all-to-all-done), channel_id=1, replica_groups=mesh['section'=2,'expert'=4,'tensor'=4] {'tensor'}, dimensions={2}, use_global_device_ids=true | all-gather | bytes 491520 | tf_op jit(solution)/shard_map/all_gather | solution.py:113
  39.1 12.0 %all_gather.13 = bf16[64,6144]{1,0:T(8,128)(2,1)S(1)} all-gather(bf16[32,6144]{1,0:T(8,128)(2,1)S(1)} %bitcast.81), channel_id=1, replica_groups=mesh['section'=2,'expert'=4,'tensor'=4] {'section'}, dimensions={0}, use_global_device_ids=true | all-gather | bytes 1179648 | tf_op jit(solution)/shard_map/all_gather | solution.py:114
  51.2 6.9 %fusion.51 = f32[64,1024]{1,0:T(8,128)S(1)} fusion(bf16[64,6144]{1,0:T(8,128)(2,1)S(1)} %all_gather.13, bf16[1,6144,1024]{2,1,0:T(8,128)(2,1)} %param.15), kind=kOutput, calls=%fused_computation.73 | convolution fusion | flops 805306368 | bytes 13631488 | tf_op jit(solution)/shard_map/dot_general | solution.py:32
  58.0 6.9 %fusion.53 = f32[64,1024]{1,0:T(8,128)S(1)} fusion(bf16[64,6144]{1,0:T(8,128)(2,1)S(1)} %all_gather.13, bf16[1,6144,1024]{2,1,0:T(8,128)(2,1)} %param.14), kind=kOutput, calls=%fused_computation.75 | convolution fusion | flops 805306368 | bytes 13631488 | tf_op jit(solution)/shard_map/dot_general | solution.py:31
  64.9 6.2 %all_gather.14 = bf16[4,8,6144]{2,1,0:T(8,128)(2,1)S(1)} all-gather(bf16[4,8,1536]{2,1,0:T(8,128)(2,1)S(1)} %all-to-all-done.2), channel_id=1, replica_groups=mesh['section'=2,'expert'=4,'tensor'=4] {'tensor'}, dimensions={2}, use_global_device_ids=true | all-gather | bytes 491520 | tf_op jit(solution)/shard_map/all_gather | solution.py:135
  71.1 12.0 %all_gather.15 = bf16[64,6144]{1,0:T(8,128)(2,1)S(1)} all-gather(bf16[32,6144]{1,0:T(8,128)(2,1)S(1)} %bitcast.82), channel_id=1, replica_groups=mesh['section'=2,'expert'=4,'tensor'=4] {'section'}, dimensions={0}, use_global_device_ids=true | all-gather | bytes 1179648 | tf_op jit(solution)/shard_map/all_gather | solution.py:136
  83.1 8.5 %multiply_convert_fusion = (bf16[64,1024]{1,0:T(8,128)(2,1)S(1)}, bf16[64,1024]{1,0:T(8,128)(2,1)S(1)}, bf16[64,1024]{1,0:T(8,128)(2,1)S(1)}) fusion(f32[64,1024]{1,0:T(8,128)S(1)} %fusion.53, f32[64,1024]{1,0:T(8,128)S(1)} %fusion.51, bf16[64,6144]{1,0:T(8,128)(2,1)S(1)} %all_gather.15, bf16[1,1024,6144]{2,1,0:T(8,128)(2,1)} %param.16), kind=kOutput, calls=%fused_computation.27 | convolution fusion | flops 806289408 | bytes 14286848 | tf_op jit(solution)/shard_map/dot_general | solution.py:60
  91.7 46.0 %while.24 = (s32[]{:T(128)}, bf16[8,32,1536]{2,1,0:T(8,128)(2,1)S(1)}, s32[8]{0:T(128)S(1)}, bf16[64,1024]{1,0:T(8,128)(2,1)S(1)}, bf16[1024,6144]{1,0:T(8,128)(...) while((s32[]{:T(128)}, ...), condition=%wide.region_5.6_spmd, body=%wide.region_4.5_spmd.sunk | while | flops 100663328 | bytes 3408324 | solution.py:117
  95.0 2.5 fusion.76
  100.7 2.5 fusion.76
  106.5 2.5 fusion.76
  112.2 2.5 fusion.76
  118.0 2.5 fusion.76
  123.7 2.5 fusion.76
  129.5 2.5 fusion.76
  135.2 2.5 fusion.76
  137.8 0.9 copy-done.2
  138.8 72.7 %while.25 = (s32[]{:T(128)}, bf16[8,32,1536]{2,1,0:T(8,128)(2,1)S(1)}, s32[8]{0:T(128)S(1)}, bf16[64,1024]{1,0:T(8,128)(2,1)S(1)}, bf16[6144,1024]{1,0:T(8,128)(...) while((s32[]{:T(128)}, ...), condition=%wide.region_9.10_spmd, body=%wide.region_8.9_spmd.sunk | while | flops 201375776 | bytes 7012828 | solution.py:140
  142.0 2.9 fusion.81
  144.9 3.0 fusion.82
  151.1 2.9 fusion.81
  154.1 2.9 fusion.82
  160.2 2.9 fusion.81
  163.1 3.0 fusion.82
  169.3 3.0 fusion.81
  172.3 2.9 fusion.82
  178.4 2.9 fusion.81
  181.4 2.9 fusion.82
  187.5 2.9 fusion.81
  190.4 2.9 fusion.82
  196.6 2.9 fusion.81
  199.5 2.9 fusion.82
  205.6 2.9 fusion.81
  208.6 2.9 fusion.82
  211.5 0.9 copy-done.1
  212.5 5.1 %all-to-all-start.1 = ((bf16[4,8,1536]{2,1,0:T(8,128)(2,1)}), bf16[4,8,1536]{2,1,0:T(8,128)(2,1)S(1)}, u32[]{:S(2)}, u32[]{:S(2)}) async-start(bf16[4,8,1536]{2,1,0:T(8,128)(2,1)} %bitcast.83), calls=%async_computation.2 | async-start | bytes 196608 | tf_op jit(solution)/shard_map/all_to_all | solution.py:127
  217.7 31.1 %reduce-scatter.5.cloned.1.call-done = bf16[32,1536]{1,0:T(8,128)(2,1)} async-done(((bf16[256,1536]{1,0:T(8,128)(2,1)}), bf16[32,1536]{1,0:T(8,128)(2,1)}) %reduce-scatter.5.cloned.1.call-update) | async-done | bytes 98320 | tf_op jit(solution)/shard_map/reduce_scatter | solution.py:139
  248.8 4.6 %all-to-all-start.3 = ((bf16[4,8,1536]{2,1,0:T(8,128)(2,1)}), bf16[4,8,1536]{2,1,0:T(8,128)(2,1)S(1)}, u32[]{:S(2)}, u32[]{:S(2)}) async-start(bf16[4,8,1536]{2,1,0:T(8,128)(2,1)} %bitcast.84), calls=%async_computation.5 | async-start | bytes 196608 | tf_op jit(solution)/shard_map/all_to_all | solution.py:150
  254.1 6.0 %psum.22 = f32[8,2]{0,1:T(2,128)S(1)} all-reduce(f32[8,2]{0,1:T(2,128)S(1)} %get-tuple-element.165), channel_id=1, replica_groups=mesh['section'=2,'expert'=4,'tensor'=4] {'tensor'}, use_global_device_ids=true, to_apply=%region_13.14 | all-reduce | flops 16 | bytes 128 | tf_op jit(solution)/shard_map/psum | solution.py:165
  260.4 38.2 %psum.23 = f32[1536,4]{0,1:T(4,128)} all-reduce(f32[1536,4]{0,1:T(4,128)S(1)} %convolution_bitcast_fusion), channel_id=1, replica_groups=mesh['section'=2,'expert'=4,'tensor'=4] {'section','expert'}, use_global_device_ids=true, to_apply=%region_15.16 | all-reduce | flops 6144 | bytes 49152 | tf_op jit(solution)/shard_map/psum | solution.py:171
  298.8 0.9 fusion.29
  (66 shorter events, 15.6 us)
Async XLA Ops:
  7.2 10.0 %copy-start = (f32[6144,4]{0,1:T(4,128)S(1)}, f32[6144,4]{0,1:T(4,128)}, u32[]{:S(2)}) copy-start(f32[6144,4]{0,1:T(4,128)} %param.13) | copy-start | bytes 294916
  10.1 18.2 %all-to-all-start = ((bf16[4,8,1536]{2,1,0:T(8,128)(2,1)}), bf16[4,8,1536]{2,1,0:T(8,128)(2,1)S(1)}, u32[]{:S(2)}, u32[]{:S(2)}) async-start(bf16[4,8,1536]{2,1,0:T(8,128)(2,1)} %fusion.27), calls=%async_computation | async-start | bytes 196608 | tf_op jit(solution)/shard_map/all_to_all | solution.py:112
  28.3 36.6 %all-to-all-start.2 = ((bf16[4,8,1536]{2,1,0:T(8,128)(2,1)}), bf16[4,8,1536]{2,1,0:T(8,128)(2,1)S(1)}, u32[]{:S(2)}, u32[]{:S(2)}) async-start(bf16[4,8,1536]{2,1,0:T(8,128)(2,1)} %fusion.28), calls=%async_computation.3 | async-start | bytes 196608 | tf_op jit(solution)/shard_map/all_to_all | solution.py:134
  32.8 179.6 %reduce-scatter.3.cloned.1.call-start = ((), (), s32[]{:S(2)}) async-start(), calls=%async_computation.6 | async-start | bytes 884736 | tf_op jit(solution)/shard_map/reduce_scatter | solution.py:116
  137.7 0.9 copy-start.2
  138.7 110.1 %reduce-scatter.5.cloned.1.call-start = ((), (), s32[]{:S(2)}) async-start(), calls=%async_computation.7 | async-start | bytes 884736 | tf_op jit(solution)/shard_map/reduce_scatter | solution.py:139
  138.8 121.4 %copy-start.4 = (s32[8,2]{0,1:T(2,128)S(1)}, s32[8,2]{0,1:T(2,128)}, u32[]{:S(2)}) copy-start(s32[8,2]{0,1:T(2,128)} %param.12) | copy-start | bytes 196
  138.8 121.4 %copy-start.3 = (bf16[8,1536]{1,0:T(8,128)(2,1)S(1)}, bf16[8,1536]{1,0:T(8,128)(2,1)}, u32[]{:S(2)}) copy-start(bf16[8,1536]{1,0:T(8,128)(2,1)} %param.11) | copy-start | bytes 73732
  211.5 0.9 copy-start.1
  212.5 36.3 %all-to-all-start.1 = ((bf16[4,8,1536]{2,1,0:T(8,128)(2,1)}), bf16[4,8,1536]{2,1,0:T(8,128)(2,1)S(1)}, u32[]{:S(2)}, u32[]{:S(2)}) async-start(bf16[4,8,1536]{2,1,0:T(8,128)(2,1)} %bitcast.83), calls=%async_computation.2 | async-start | bytes 196608 | tf_op jit(solution)/shard_map/all_to_all | solution.py:127
  248.8 49.9 %all-to-all-start.3 = ((bf16[4,8,1536]{2,1,0:T(8,128)(2,1)}), bf16[4,8,1536]{2,1,0:T(8,128)(2,1)S(1)}, u32[]{:S(2)}, u32[]{:S(2)}) async-start(bf16[4,8,1536]{2,1,0:T(8,128)(2,1)} %bitcast.84), calls=%async_computation.5 | async-start | bytes 196608 | tf_op jit(solution)/shard_map/all_to_all | solution.py:150
Sparse Core Ops, SparseCore 0:
  138.8 36.1 reduce-scatter.2
  212.6 36.1 reduce-scatter.4
where the time goes:
time: 309 us; the launch traced here: 306 us
  matrix products  94.1 us (30%)
  blocking collectives  87.4 us (28%)
  loops' own time  42 us (14%)
  waiting for transfers between devices  31.1 us (10%)
  starting transfers between devices  20.6 us (7%)
  local copies, waits for them, and re-layouts  14.4 us (5%)
  between operations  14.2 us (5%)
    dot_general x17, matrix products, contract_last(): lax.dot_general(left, right, (((1,), (1,)), ((), ())), preferred_element_...  55.4 us
    psum x1, blocking collectives, on_device(): grad_router = lax.psum(router_part, ('section', 'expert'))  38.2 us
    reduce_scatter x1, waiting for transfers between devices, on_device(): lax.psum_scatter(lax.map(lambda block: backward_block(grad_gate, grad_up,...  31.1 us
    another operation x1, loops' own time, on_device(): lax.map(lambda block: backward_block(grad_gate, grad_up, block), block_id...  21 us
    another operation x1, loops' own time, on_device(): lax.map(lambda block: forward_block(hidden, block), block_ids(lax.axis_si...  21 us
    dot_general x8, matrix products, forward_block(): return jnp.dot(hidden_rows, columns, preferred_element_type=jnp.float32)  20.3 us
    all_gather x1, blocking collectives, on_device(): lax.all_gather(landed_x.reshape(block_rows, -1), 'section', axis=0, tiled...  12 us
    all_gather x1, blocking collectives, on_device(): lax.all_gather(landed_dy.reshape(block_rows, -1), 'section', axis=0, tile...  12 us
  transfers between devices with their start and end apart: 6, of which 1 were waited for; matrix products, arithmetic and copies ran while one was open for 23% of the time, Pallas kernels for 0%

commit v1 on v0

v1 whole, which is shorter than its diff:
```python
import functools

import jax
import jax.numpy as jnp
from jax import lax
from jax.experimental import pallas as pl
from jax.experimental.pallas import tpu as pltpu
from jax.sharding import PartitionSpec as P

F32 = jnp.float32
BF16 = jnp.bfloat16
LANES = 128
precise = lax.Precision.HIGHEST


def contract_last(left, right):
    return lax.dot_general(left, right, (((1,), (1,)), ((), ())), preferred_element_type=F32)


def step_of(size, most):
    step = most
    while size % step:
        step //= 2
    return step


def layer_kernel(
    sizes,
    tokens_ref,
    routes_ref,
    router_ref,
    grad_out_ref,
    gate_hbm,
    up_hbm,
    down_hbm,
    moe_ref,
    grad_tokens_ref,
    grad_router_ref,
    gate,
    up,
    down,
    gathered,
    xs,
    dys,
    router_parts,
    router_pad,
    logits,
    acc_gate,
    acc_up,
    acc_down,
    hidden,
    grad_gate,
    grad_up,
    weight_own,
    from_sibling,
    from_plane,
    plane_sum,
    from_expert,
    gw_own,
    gw_plane,
    gw_expert,
    grad_logits,
    weight_sems,
    send_sems,
    recv_sems,
):
    sections, experts, tensors, quarter, ff_dev = sizes
    half = tensors // 2
    plane = sections * half
    groups = sections * experts
    count = groups * 8
    section = lax.axis_index("section")
    expert = lax.axis_index("expert")
    tensor = lax.axis_index("tensor")
    row = tensor // 2
    core = tensor % 2
    group = section * experts + expert
    here = {"section": section, "expert": expert, "tensor": tensor}

    def at(**moved):
        return {**here, **moved}

    def expert_peer(k):
        return at(expert=(expert + k) % experts)

    def plane_peer(k):
        return at(
            section=(section + k // half) % sections,
            tensor=((row + k % half) % half) * 2 + core,
        )

    sibling = at(tensor=row * 2 + 1 - core)
    used = [0]
    sends = []

    def remote(src, dst, peer):
        index = used[0]
        used[0] += 1
        copy = pltpu.make_async_remote_copy(
            src_ref=src,
            dst_ref=dst,
            send_sem=send_sems.at[index],
            recv_sem=recv_sems.at[index],
            device_id=peer,
            device_id_type=pl.DeviceIdType.MESH,
        )
        copy.start()
        sends.append(copy)
        return copy

    barrier = pltpu.get_barrier_semaphore()
    peers = (
        [expert_peer(k) for k in range(1, experts)]
        + [plane_peer(k) for k in range(1, plane)]
        + [sibling]
    )
    for peer in peers:
        pl.semaphore_signal(barrier, inc=1, device_id=peer, device_id_type=pl.DeviceIdType.MESH)

    def quarter_at(dy, other):
        return ((row + half - dy) % half) * 2 + (1 - core if other else core)

    order = [quarter_at(dy, other) for dy in range(half) for other in (False, True)]
    weight_copies = []
    for j, q in enumerate(order):
        span = pl.ds(pl.multiple_of(q * quarter, LANES), quarter)
        trio = [
            pltpu.make_async_copy(gate_hbm.at[span, :], gate.at[span, :], weight_sems.at[j, 0]),
            pltpu.make_async_copy(up_hbm.at[span, :], up.at[span, :], weight_sems.at[j, 1]),
            pltpu.make_async_copy(down_hbm.at[:, span], down.at[:, span], weight_sems.at[j, 2]),
        ]
        for copy in trio:
            copy.start()
        weight_copies.append(trio)

    lane8 = lax.broadcasted_iota(jnp.int32, (8, LANES), 1)
    routes = routes_ref[...]
    hot = jnp.zeros((8, LANES), F32)
    for k in range(routes.shape[1]):
        hot = jnp.where(routes[:, k : k + 1] == lane8, 1.0, hot)
    unit_rows = pl.ds(pl.multiple_of(group * 16, 16), 16)
    gathered[tensor, unit_rows, 0:quarter] = jnp.concatenate(
        [tokens_ref[...].astype(F32), grad_out_ref[...].astype(F32)], axis=0
    ).astype(BF16)
    gathered[tensor, unit_rows, quarter : quarter + LANES] = jnp.concatenate(
        [hot, jnp.zeros((8, LANES), F32)], axis=0
    ).astype(BF16)

    pl.semaphore_wait(barrier, len(peers))

    unit = gathered.at[tensor, unit_rows, :]
    over_expert = [remote(unit, unit, expert_peer(k)) for k in range(1, experts)]

    router_pad[...] = jnp.zeros_like(router_pad)
    router_pad[0:experts, :] = router_ref[...]
    wide = router_pad[...]
    high = wide.astype(BF16).astype(F32)
    middle = (wide - high).astype(BF16).astype(F32)
    low = wide - high - middle
    router_parts[...] = jnp.zeros_like(router_parts)
    router_parts[0:32, :] = jnp.concatenate(
        [high, middle, low, jnp.zeros_like(low)], axis=0
    ).astype(BF16)
    logits[...] = jnp.zeros_like(logits)
    acc_gate[...] = jnp.zeros_like(acc_gate)
    acc_up[...] = jnp.zeros_like(acc_up)
    acc_down[...] = jnp.zeros_like(acc_down)
    gw_own[...] = jnp.zeros_like(gw_own)

    for copy in over_expert:
        copy.wait_recv()

    def chunk_of(k):
        from_section = (section + sections - k // half) % sections
        from_tensor = quarter_at(k % half, False)
        rows = pl.ds(pl.multiple_of(from_section * experts * 16, 16), experts * 16)
        return gathered.at[from_tensor, rows, :]

    own_chunk = chunk_of(0)
    over_plane = {k: remote(own_chunk, own_chunk, plane_peer(k)) for k in range(1, plane)}
    over_core = {0: remote(own_chunk, own_chunk, sibling)}
    by_row = sorted(range(1, plane), key=lambda k: (k % half, k // half))
    for k in by_row:
        over_plane[k].wait_recv()
        over_core[k] = remote(chunk_of(k), chunk_of(k), sibling)

    gather_sends = len(sends)
    tile = step_of(ff_dev, 256)
    for j, q in enumerate(order):
        dy = j // 2
        if j % 2 == 1:
            for k in range(plane):
                if k % half == dy:
                    over_core[k].wait_recv()

        @pl.loop(0, groups // 2)
        def _(pair):
            rows = pl.ds(pl.multiple_of(pair * 16, 16), 16)
            block = gathered[
                q, pl.ds(pl.multiple_of(pair * 32, 16), 32), 0:quarter
            ].astype(F32)
            xs[q, rows, :] = jnp.concatenate([block[0:8], block[16:24]], axis=0).astype(BF16)
            dys[rows, :] = jnp.concatenate([block[8:16], block[24:32]], axis=0).astype(BF16)

        x = xs[q]
        dy_rows = dys[...]
        span = pl.ds(pl.multiple_of(q * quarter, LANES), quarter)
        logits[...] += contract_last(x, router_parts[:, span])
        for copy in weight_copies[j]:
            copy.wait()

        @pl.loop(0, ff_dev // tile)
        def _(n):
            cols = pl.ds(pl.multiple_of(n * tile, tile), tile)
            acc_gate[:, cols] += jnp.dot(x, gate[span, cols], preferred_element_type=F32)
            acc_up[:, cols] += jnp.dot(x, up[span, cols], preferred_element_type=F32)
            acc_down[:, cols] += contract_last(dy_rows, down[cols, span])

    lane = lax.broadcasted_iota(jnp.int32, (count, LANES), 1)
    meta = gathered[tensor, :, quarter : quarter + LANES].astype(F32)
    mask = jnp.concatenate([meta[16 * g : 16 * g + 8] for g in range(groups)], axis=0)
    parts = logits[...]
    summed = jnp.zeros((count, LANES), F32)
    for b in range(experts):
        column = jnp.sum(jnp.where(lane % 8 == b, parts, 0.0), axis=1, keepdims=True)
        summed = jnp.where(lane == b, column, summed)
    scores = jnp.where(mask > 0.5, jax.nn.sigmoid(summed), 0.0)
    totals = jnp.sum(scores, axis=1, keepdims=True)
    weights = scores / totals
    is_own = lane == expert
    weight_own[...] = jnp.broadcast_to(
        jnp.sum(jnp.where(is_own, weights, 0.0), axis=1, keepdims=True), (count, LANES)
    )

    @pl.loop(0, ff_dev // tile)
    def _(n):
        cols = pl.ds(pl.multiple_of(n * tile, tile), tile)
        pre_gate = acc_gate[:, cols]
        pre_up = acc_up[:, cols]
        plain = acc_down[:, cols]
        sig = jax.nn.sigmoid(pre_gate)
        act = pre_gate * sig
        hid = (act * pre_up).astype(BF16)
        hidden[:, cols] = hid
        grad_hidden = plain * weight_own[:, 0:1]
        grad_gate[:, cols] = (grad_hidden * pre_up * sig * (1.0 + pre_gate * (1.0 - sig))).astype(
            BF16
        )
        grad_up[:, cols] = (grad_hidden * act).astype(BF16)
        term = jnp.sum(hid.astype(F32) * plain, axis=1, keepdims=True)
        gw_own[0] += jnp.where(is_own, term, 0.0)

    gw_core = remote(gw_own.at[0], gw_own.at[3], sibling)

    for copy in sends[:gather_sends]:
        copy.wait_send()
    partial = gathered
    wide_tile = step_of(quarter, 512)

    def back(q, slot, added):
        h, gg, gu = hidden[...], grad_gate[...], grad_up[...]
        scale = weight_own[:, 0:1]

        @pl.loop(0, quarter // wide_tile)
        def _(n):
            cols = pl.ds(pl.multiple_of(n * wide_tile, LANES), wide_tile)
            span = pl.ds(pl.multiple_of(q * quarter + n * wide_tile, LANES), wide_tile)
            out = jnp.dot(h, down[:, span], preferred_element_type=F32) * scale
            grad = contract_last(gg, gate[span, :]) + contract_last(gu, up[span, :])
            for g in range(groups):
                both = jnp.concatenate([out[8 * g : 8 * g + 8], grad[8 * g : 8 * g + 8]], axis=0)
                if added is not None:
                    both = both + from_sibling[added, 16 * g : 16 * g + 16, cols].astype(F32)
                partial[slot, 16 * g : 16 * g + 16, cols] = both.astype(BF16)

    outer = list(range(1, half)) + [0]

    def target_at(dy, other):
        return ((row + dy) % half) * 2 + (1 - core if other else core)

    to_core = {}
    gw_over_plane = gw_over_expert = None
    for place, dy in enumerate(outer):
        back(target_at(dy, True), dy * 2 + 1, None)
        to_core[dy] = remote(partial.at[dy * 2 + 1, :, 0:quarter], from_sibling.at[dy], sibling)
        if place == 0:
            gw_core.wait_recv()
            gw_own[1] = gw_own[0] + gw_own[3]
            gw_over_plane = [
                remote(gw_own.at[1], gw_plane.at[k - 1], plane_peer(k)) for k in range(1, plane)
            ]
    for copy in gw_over_plane:
        copy.wait_recv()
    total = gw_own[1]
    for k in range(1, plane):
        total = total + gw_plane[k - 1]
    gw_own[2] = total
    gw_over_expert = [
        remote(gw_own.at[2], gw_expert.at[k - 1], expert_peer(k)) for k in range(1, experts)
    ]

    to_plane = {}
    for dy in outer:
        to_core[dy].wait_recv()
        back(target_at(dy, False), dy * 2, dy)
        for ds in range(sections):
            k = ds * half + dy
            if k:
                first = pl.multiple_of(((section + ds) % sections) * experts * 16, 16)
                to_plane[k] = remote(
                    partial.at[dy * 2, pl.ds(first, experts * 16), 0:quarter],
                    from_plane.at[k - 1],
                    plane_peer(k),
                )

    for copy in gw_over_expert:
        copy.wait_recv()
    grad_weight = gw_own[2]
    for k in range(1, experts):
        grad_weight = grad_weight + gw_expert[k - 1]
    cross = jnp.zeros((count, LANES), F32)
    for b in range(experts):
        is_b = lane == b
        other_score = jnp.sum(jnp.where(is_b, scores, 0.0), axis=1, keepdims=True)
        other_grad = jnp.sum(jnp.where(is_b, grad_weight, 0.0), axis=1, keepdims=True)
        cross = cross + jnp.where(is_b, 0.0, (grad_weight - other_grad) * other_score)
    grad_chosen = cross / (totals * totals) * scores * (1.0 - scores)
    grad_logits[...] = jnp.where(mask > 0.5, grad_chosen, 0.0)
    turned = grad_logits[...].T
    grad_router_ref[...] = jnp.dot(
        turned[0:8], xs[tensor].astype(F32), precision=precise, preferred_element_type=F32
    )[0:experts]
    own_rows = pl.ds(pl.multiple_of(group * 8, 8), 8)
    own_span = pl.ds(pl.multiple_of(tensor * quarter, LANES), quarter)
    through_router = jnp.dot(
        grad_logits[own_rows, 0:8],
        router_pad[:, own_span],
        precision=precise,
        preferred_element_type=F32,
    )

    for k in sorted(to_plane, key=lambda k: (-(k % half), k)):
        to_plane[k].wait_recv()
    own_section = pl.multiple_of(section * experts * 16, 16)

    @pl.loop(0, experts)
    def _(e):
        rows = pl.ds(pl.multiple_of(e * 16, 16), 16)
        home = pl.ds(pl.multiple_of(own_section + e * 16, 16), 16)
        value = partial[0, home, 0:quarter].astype(F32)
        for k in range(1, plane):
            value = value + from_plane[k - 1, rows, :].astype(F32)
        plane_sum[rows, :] = value.astype(BF16)

    back_home = []
    for k in range(1, experts):
        first = pl.multiple_of(((expert + k) % experts) * 16, 16)
        back_home.append(
            remote(plane_sum.at[pl.ds(first, 16), :], from_expert.at[k - 1], expert_peer(k))
        )
    value = plane_sum[pl.ds(pl.multiple_of(expert * 16, 16), 16), :].astype(F32)
    for k in range(1, experts):
        back_home[k - 1].wait_recv()
        value = value + from_expert[k - 1].astype(F32)
    moe_ref[...] = value[0:8].astype(BF16)
    grad_tokens_ref[...] = (value[8:16] + through_router).astype(BF16)

    for copy in sends[gather_sends:]:
        copy.wait_send()


def on_device(tokens, routes, router, gate_proj, up_proj, down_proj, grad_out):
    sections = lax.axis_size("section")
    experts = lax.axis_size("expert")
    tensors = lax.axis_size("tensor")
    quarter = tokens.shape[1]
    width = router.shape[0]
    ff_dev = gate_proj.shape[2]
    half = tensors // 2
    plane = sections * half
    groups = sections * experts
    count = groups * 8
    copies = 3 * (experts - 1) + 3 * (plane - 1) + plane + half + 1
    vmem = pl.BlockSpec(memory_space=pltpu.VMEM)
    hbm = pl.BlockSpec(memory_space=pl.ANY)
    moe_out, grad_tokens, grad_router = pl.pallas_call(
        functools.partial(layer_kernel, (sections, experts, tensors, quarter, ff_dev)),
        out_shape=(
            jax.ShapeDtypeStruct(tokens.shape, BF16),
            jax.ShapeDtypeStruct(tokens.shape, BF16),
            jax.ShapeDtypeStruct((experts, quarter), F32),
        ),
        in_specs=[vmem] * 4 + [hbm] * 3,
        out_specs=(vmem, vmem, vmem),
        scratch_shapes=[
            pltpu.VMEM((width, ff_dev), BF16),
            pltpu.VMEM((width, ff_dev), BF16),
            pltpu.VMEM((ff_dev, width), BF16),
            pltpu.VMEM((tensors, groups * 16, quarter + LANES), BF16),
            pltpu.VMEM((tensors, count, quarter), BF16),
            pltpu.VMEM((count, quarter), BF16),
            pltpu.VMEM((LANES, width), BF16),
            pltpu.VMEM((8, width), F32),
            pltpu.VMEM((count, LANES), F32),
            pltpu.VMEM((count, ff_dev), F32),
            pltpu.VMEM((count, ff_dev), F32),
            pltpu.VMEM((count, ff_dev), F32),
            pltpu.VMEM((count, ff_dev), BF16),
            pltpu.VMEM((count, ff_dev), BF16),
            pltpu.VMEM((count, ff_dev), BF16),
            pltpu.VMEM((count, LANES), F32),
            pltpu.VMEM((half, groups * 16, quarter), BF16),
            pltpu.VMEM((plane - 1, experts * 16, quarter), BF16),
            pltpu.VMEM((experts * 16, quarter), BF16),
            pltpu.VMEM((experts - 1, 16, quarter), BF16),
            pltpu.VMEM((4, count, LANES), F32),
            pltpu.VMEM((plane - 1, count, LANES), F32),
            pltpu.VMEM((experts - 1, count, LANES), F32),
            pltpu.VMEM((count, LANES), F32),
            pltpu.SemaphoreType.DMA((tensors, 3)),
            pltpu.SemaphoreType.DMA((copies,)),
            pltpu.SemaphoreType.DMA((copies,)),
        ],
        compiler_params=pltpu.CompilerParams(
            collective_id=0, has_side_effects=True, vmem_limit_bytes=58 * 1024 * 1024
        ),
    )(tokens, routes, router.T, grad_out, gate_proj[0], up_proj[0], down_proj[0])
    return (moe_out, grad_tokens, grad_router.T)


def solution(mesh):
    return jax.shard_map(
        on_device,
        mesh=mesh,
        in_specs=(
            P(("section", "expert"), "tensor"),
            P(("section", "expert"), None),
            P(),
            P("expert", None, ("section", "tensor")),
            P("expert", None, ("section", "tensor")),
            P("expert", ("section", "tensor"), None),
            P(("section", "expert"), "tensor"),
        ),
        out_specs=(
            P(("section", "expert"), "tensor"),
            P(("section", "expert"), "tensor"),
            P("tensor", None),
        ),
        check_vma=False,
    )
```

time: 309 us -> 64.9 us (0.21)
  matrix products: 94.1 us -> 0 us
  blocking collectives: 87.4 us -> 0 us
  Pallas kernels: 0 us -> 58.5 us
  loops' own time: 42 us -> 0 us
  waiting for transfers between devices: 31.1 us -> 0 us
  starting transfers between devices: 20.6 us -> 0 us
  between operations: 14.2 us -> 0.64 us
  local copies, waits for them, and re-layouts: 14.4 us -> 5.38 us
    dot_general x34 -> x0, matrix products: 94.1 us -> none  [the longest x17 55.4 us: contract_last(): lax.dot_general(left, right, (((1,), (1,)), ((), ())), preferred_element_...]
    pallas_call x0 -> x1, Pallas kernels: none -> 58.5 us  [on_device(): pl.pallas_call(functools.partial(layer_kernel, (sections, experts, tensor...]
    psum x3 -> x0, blocking collectives: 50.9 us -> none  [the longest x1 38.2 us: on_device(): grad_router = lax.psum(router_part, ('section', 'expert'))]
    another operation x2 -> x0, loops' own time: 42 us -> none  [the longest x1 21 us: on_device(): lax.map(lambda block: backward_block(grad_gate, grad_up, block), block_id...]
    all_gather x4 -> x0, blocking collectives: 36.5 us -> none  [the longest x1 12 us: on_device(): lax.all_gather(landed_x.reshape(block_rows, -1), 'section', axis=0, tiled...]
    reduce_scatter x2 -> x0, waiting for transfers between devices: 31.1 us -> none  [the longest x1 31.1 us: on_device(): lax.psum_scatter(lax.map(lambda block: backward_block(grad_gate, grad_up,...]
    all_to_all x4 -> x0, starting transfers between devices: 20.6 us -> none  [the longest x1 6.32 us: on_device(): lax.all_to_all(x_sent, 'expert', split_axis=0, concat_axis=0, tiled=True)]
    dynamic_slice x16 -> x0, local copies, waits for them, and re-layouts: 9.52 us -> none  [on_device(): lax.map(lambda block: forward_block(hidden, block), block_ids(lax.axis_si...]
  transfers between devices with their start and end apart: 6 -> 0, of which waited for: 1 -> 0; matrix products, arithmetic and copies ran while one was open for 23% -> 0% of each run, Pallas kernels for 0% -> 0%
where the time goes in v1:
time: 64.9 us; the launch traced here: 64.5 us
  Pallas kernels  58.5 us (90%)
  local copies, waits for them, and re-layouts  5.38 us (8%)
    pallas_call x1, Pallas kernels, on_device(): pl.pallas_call(functools.partial(layer_kernel, (sections, experts, tensor...  58.5 us
    unnamed x4, local copies, waits for them, and re-layouts  5.38 us

profile of v1, /device:TPU:0, one launch (start us, length us, event | category | flops | bytes accessed | tf_op | source)
XLA Modules:
  0.0 64.5 jit_solution(2731235996491287819)
XLA Ops:
  0.6 1.3 %copy.10.routes_ref = s32[8,2]{1,0:T(8,128)} copy(s32[8,2]{0,1:T(2,128)} %param.8) | data formatting | bytes 128 | tf_op args[1]
  2.0 58.5 %shard_map.94 = (bf16[8,1536]{1,0:T(8,128)(2,1)}, bf16[8,1536]{1,0:T(8,128)(2,1)}, f32[4,1536]{1,0:T(4,128)}) custom-call(bf16[8,1536]{1,0:T(8,128)(2,1)} %tokens_ref.1, s32[8,2]{1,0:T(8,128)} %copy.10.routes_ref, f32[4,6144]{1,0:T(4,128)} %bitcast.8, bf16[8,1536]{1,0:T(8,128)(2,1)} %grad_out_ref.1, bf16[6144,1024]{1,0:T(8,128)(2,1)} %bitcast.5, ...), custom_call_target="tpu_custom_call" | custom-call | tf_op jit(solution)/shard_map/pallas_call | solution.py:386
  60.5 1.3 %copy.14 = bf16[8,1536]{1,0:T(8,128)(2,1)} copy(bf16[8,1536]{1,0:T(8,128)(2,1)} %get-tuple-element.12) | data formatting | bytes 49152
  61.8 1.3 %copy.15 = bf16[8,1536]{1,0:T(8,128)(2,1)} copy(bf16[8,1536]{1,0:T(8,128)(2,1)} %get-tuple-element.13) | data formatting | bytes 49152
  63.2 1.3 %copy.16 = f32[1536,4]{0,1:T(4,128)} copy(f32[1536,4]{0,1:T(4,128)} %bitcast.9) | data formatting | bytes 49152

commit v2 on v1

--- a/solution.py
+++ b/solution.py
@@ -134,10 +134,14 @@
         weight_copies.append(trio)
 
     lane8 = lax.broadcasted_iota(jnp.int32, (8, LANES), 1)
-    routes = routes_ref[...]
+    routes = routes_ref[...].astype(F32)
+    diagonal = lax.broadcasted_iota(jnp.int32, (8, 8), 0) == lax.broadcasted_iota(
+        jnp.int32, (8, 8), 1
+    )
     hot = jnp.zeros((8, LANES), F32)
-    for k in range(routes.shape[1]):
-        hot = jnp.where(routes[:, k : k + 1] == lane8, 1.0, hot)
+    for k in range(routes.shape[0]):
+        column = jnp.sum(jnp.where(diagonal, routes[k : k + 1, :], 0.0), axis=1, keepdims=True)
+        hot = jnp.where(column == lane8.astype(F32), 1.0, hot)
     unit_rows = pl.ds(pl.multiple_of(group * 16, 16), 16)
     gathered[tensor, unit_rows, 0:quarter] = jnp.concatenate(
         [tokens_ref[...].astype(F32), grad_out_ref[...].astype(F32)], axis=0
@@ -149,7 +153,10 @@
     pl.semaphore_wait(barrier, len(peers))
 
     unit = gathered.at[tensor, unit_rows, :]
-    over_expert = [remote(unit, unit, expert_peer(k)) for k in range(1, experts)]
+    over_expert = {k: remote(unit, unit, expert_peer(k)) for k in range(1, experts)}
+    near = [k for k in range(1, plane) if k % half == 0]
+    far = sorted([k for k in range(1, plane) if k % half], key=lambda k: (k % half, k // half))
+    over_plane = {(k, 0): remote(unit, unit, plane_peer(k)) for k in near + far}
 
     router_pad[...] = jnp.zeros_like(router_pad)
     router_pad[0:experts, :] = router_ref[...]
@@ -167,8 +174,12 @@
     acc_down[...] = jnp.zeros_like(acc_down)
     gw_own[...] = jnp.zeros_like(gw_own)
 
-    for copy in over_expert:
-        copy.wait_recv()
+    for j in sorted(range(1, experts), key=lambda j: (min(j, experts - j), j)):
+        over_expert[j].wait_recv()
+        first = (section * experts + (expert + experts - j) % experts) * 16
+        landed = gathered.at[tensor, pl.ds(pl.multiple_of(first, 16), 16), :]
+        for k in near + far:
+            over_plane[k, j] = remote(landed, landed, plane_peer(k))
 
     def chunk_of(k):
         from_section = (section + sections - k // half) % sections
@@ -176,18 +187,22 @@
         rows = pl.ds(pl.multiple_of(from_section * experts * 16, 16), experts * 16)
         return gathered.at[from_tensor, rows, :]
 
-    own_chunk = chunk_of(0)
-    over_plane = {k: remote(own_chunk, own_chunk, plane_peer(k)) for k in range(1, plane)}
-    over_core = {0: remote(own_chunk, own_chunk, sibling)}
-    by_row = sorted(range(1, plane), key=lambda k: (k % half, k // half))
-    for k in by_row:
-        over_plane[k].wait_recv()
+    over_core = {0: remote(chunk_of(0), chunk_of(0), sibling)}
+
+    def hand_on(k):
+        for j in range(experts):
+            over_plane[k, j].wait_recv()
         over_core[k] = remote(chunk_of(k), chunk_of(k), sibling)
 
-    gather_sends = len(sends)
+    for k in near:
+        hand_on(k)
+
     tile = step_of(ff_dev, 256)
     for j, q in enumerate(order):
         dy = j // 2
+        if j == 1:
+            for k in far:
+                hand_on(k)
         if j % 2 == 1:
             for k in range(plane):
                 if k % half == dy:
@@ -215,6 +230,8 @@
             acc_gate[:, cols] += jnp.dot(x, gate[span, cols], preferred_element_type=F32)
             acc_up[:, cols] += jnp.dot(x, up[span, cols], preferred_element_type=F32)
             acc_down[:, cols] += contract_last(dy_rows, down[cols, span])
+
+    gather_sends = len(sends)
 
     lane = lax.broadcasted_iota(jnp.int32, (count, LANES), 1)
     meta = gathered[tensor, :, quarter : quarter + LANES].astype(F32)
@@ -257,21 +274,25 @@
     partial = gathered
     wide_tile = step_of(quarter, 512)
 
+    tiles = quarter // wide_tile
+
+    def back_tile(q, slot, added, n):
+        cols = pl.ds(pl.multiple_of(n * wide_tile, LANES), wide_tile)
+        span = pl.ds(pl.multiple_of(q * quarter + n * wide_tile, LANES), wide_tile)
+        out = jnp.dot(hidden[...], down[:, span], preferred_element_type=F32)
+        out = out * weight_own[:, 0:1]
+        grad = contract_last(grad_gate[...], gate[span, :])
+        grad = grad + contract_last(grad_up[...], up[span, :])
+        for g in range(groups):
+            both = jnp.concatenate([out[8 * g : 8 * g + 8], grad[8 * g : 8 * g + 8]], axis=0)
+            if added is not None:
+                both = both + from_sibling[added, 16 * g : 16 * g + 16, cols].astype(F32)
+            partial[slot, 16 * g : 16 * g + 16, cols] = both.astype(BF16)
+
     def back(q, slot, added):
-        h, gg, gu = hidden[...], grad_gate[...], grad_up[...]
-        scale = weight_own[:, 0:1]
-
-        @pl.loop(0, quarter // wide_tile)
+        @pl.loop(0, tiles)
         def _(n):
-            cols = pl.ds(pl.multiple_of(n * wide_tile, LANES), wide_tile)
-            span = pl.ds(pl.multiple_of(q * quarter + n * wide_tile, LANES), wide_tile)
-            out = jnp.dot(h, down[:, span], preferred_element_type=F32) * scale
-            grad = contract_last(gg, gate[span, :]) + contract_last(gu, up[span, :])
-            for g in range(groups):
-                both = jnp.concatenate([out[8 * g : 8 * g + 8], grad[8 * g : 8 * g + 8]], axis=0)
-                if added is not None:
-                    both = both + from_sibling[added, 16 * g : 16 * g + 16, cols].astype(F32)
-                partial[slot, 16 * g : 16 * g + 16, cols] = both.astype(BF16)
+            back_tile(q, slot, added, n)
 
     outer = list(range(1, half)) + [0]
 
@@ -299,19 +320,58 @@
         remote(gw_own.at[2], gw_expert.at[k - 1], expert_peer(k)) for k in range(1, experts)
     ]
 
+    def section_rows(ds):
+        first = pl.multiple_of(((section + ds) % sections) * experts * 16, 16)
+        return pl.ds(first, experts * 16)
+
     to_plane = {}
-    for dy in outer:
+    for dy in outer[:-1]:
         to_core[dy].wait_recv()
         back(target_at(dy, False), dy * 2, dy)
         for ds in range(sections):
             k = ds * half + dy
-            if k:
-                first = pl.multiple_of(((section + ds) % sections) * experts * 16, 16)
-                to_plane[k] = remote(
-                    partial.at[dy * 2, pl.ds(first, experts * 16), 0:quarter],
-                    from_plane.at[k - 1],
-                    plane_peer(k),
-                )
+            to_plane[k] = remote(
+                partial.at[dy * 2, section_rows(ds), 0:quarter],
+                from_plane.at[k - 1],
+                plane_peer(k),
+            )
+
+    to_core[0].wait_recv()
+    spans = [slice(n * wide_tile, (n + 1) * wide_tile) for n in range(tiles)]
+    for n, cols in enumerate(spans):
+        back_tile(target_at(0, False), 0, 0, n)
+        for ds in range(1, sections):
+            k = ds * half
+            to_plane[k, n] = remote(
+                partial.at[0, section_rows(ds), cols],
+                from_plane.at[k - 1, :, cols],
+                plane_peer(k),
+            )
+
+    for k in far:
+        to_plane[k].wait_recv()
+    own_section = pl.multiple_of(section * experts * 16, 16)
+    back_home = {}
+    for n, cols in enumerate(spans):
+        for k in near:
+            to_plane[k, n].wait_recv()
+
+        @pl.loop(0, experts)
+        def _(e):
+            rows = pl.ds(pl.multiple_of(e * 16, 16), 16)
+            home = pl.ds(pl.multiple_of(own_section + e * 16, 16), 16)
+            value = partial[0, home, cols].astype(F32)
+            for k in range(1, plane):
+                value = value + from_plane[k - 1, rows, cols].astype(F32)
+            plane_sum[rows, cols] = value.astype(BF16)
+
+        for k in range(1, experts):
+            first = pl.multiple_of(((expert + k) % experts) * 16, 16)
+            back_home[k, n] = remote(
+                plane_sum.at[pl.ds(first, 16), cols],
+                from_expert.at[k - 1, :, cols],
+                expert_peer(k),
+            )
 
     for copy in gw_over_expert:
         copy.wait_recv()
@@ -339,34 +399,22 @@
         preferred_element_type=F32,
     )
 
-    for k in sorted(to_plane, key=lambda k: (-(k % half), k)):
-        to_plane[k].wait_recv()
-    own_section = pl.multiple_of(section * experts * 16, 16)
-
-    @pl.loop(0, experts)
-    def _(e):
-        rows = pl.ds(pl.multiple_of(e * 16, 16), 16)
-        home = pl.ds(pl.multiple_of(own_section + e * 16, 16), 16)
-        value = partial[0, home, 0:quarter].astype(F32)
-        for k in range(1, plane):
-            value = value + from_plane[k - 1, rows, :].astype(F32)
-        plane_sum[rows, :] = value.astype(BF16)
-
-    back_home = []
+    value = plane_sum[pl.ds(pl.multiple_of(expert * 16, 16), 16), :].astype(F32)
+    for copy in back_home.values():
+        copy.wait_recv()
     for k in range(1, experts):
-        first = pl.multiple_of(((expert + k) % experts) * 16, 16)
-        back_home.append(
-            remote(plane_sum.at[pl.ds(first, 16), :], from_expert.at[k - 1], expert_peer(k))
-        )
-    value = plane_sum[pl.ds(pl.multiple_of(expert * 16, 16), 16), :].astype(F32)
-    for k in range(1, experts):
-        back_home[k - 1].wait_recv()
         value = value + from_expert[k - 1].astype(F32)
     moe_ref[...] = value[0:8].astype(BF16)
     grad_tokens_ref[...] = (value[8:16] + through_router).astype(BF16)
 
     for copy in sends[gather_sends:]:
         copy.wait_send()
+
+
+def hand_over_kernel(moe_ref, tokens_ref, router_ref, moe_out, tokens_out, router_out):
+    moe_out[...] = moe_ref[...]
+    tokens_out[...] = tokens_ref[...]
+    router_out[...] = router_ref[...]
 
 
 def on_device(tokens, routes, router, gate_proj, up_proj, down_proj, grad_out):
@@ -380,7 +428,10 @@
     plane = sections * half
     groups = sections * experts
     count = groups * 8
-    copies = 3 * (experts - 1) + 3 * (plane - 1) + plane + half + 1
+    tiles = quarter // step_of(quarter, 512)
+    near = sections - 1
+    copies = (2 + tiles) * (experts - 1) + (1 + experts) * (plane - 1) + plane + half + 1
+    copies += plane - 1 - near + tiles * near
     vmem = pl.BlockSpec(memory_space=pltpu.VMEM)
     hbm = pl.BlockSpec(memory_space=pl.ANY)
     moe_out, grad_tokens, grad_router = pl.pallas_call(
@@ -424,7 +475,16 @@
         compiler_params=pltpu.CompilerParams(
             collective_id=0, has_side_effects=True, vmem_limit_bytes=58 * 1024 * 1024
         ),
-    )(tokens, routes, router.T, grad_out, gate_proj[0], up_proj[0], down_proj[0])
+    )(tokens, routes.T, router.T, grad_out, gate_proj[0], up_proj[0], down_proj[0])
+    moe_out, grad_tokens, grad_router = pl.pallas_call(
+        hand_over_kernel,
+        out_shape=tuple(
+            jax.ShapeDtypeStruct(part.shape, part.dtype)
+            for part in (moe_out, grad_tokens, grad_router)
+        ),
+        in_specs=[vmem] * 3,
+        out_specs=(vmem, vmem, vmem),
+    )(moe_out, grad_tokens, grad_router)
     return (moe_out, grad_tokens, grad_router.T)
 
 

time: 64.9 us -> 57.2 us (0.88)
  local copies, waits for them, and re-layouts: 5.38 us -> 0 us
  Pallas kernels: 58.5 us -> 56.3 us
    unnamed x4 -> x0, local copies, waits for them, and re-layouts: 5.38 us -> none
    pallas_call x1, Pallas kernels: 58.5 us -> 54.9 us  [on_device(): pl.pallas_call(functools.partial(layer_kernel, (sections, experts, tensor...]
    pallas_call x0 -> x1, Pallas kernels: none -> 1.4 us  [on_device(): pl.pallas_call(hand_over_kernel, out_shape=tuple((jax.ShapeDtypeStruct(pa...]
where the time goes in v2:
time: 57.2 us; the launch traced here: 57 us
  Pallas kernels  56.3 us (98%)
  between operations  0.64 us (1%)
    pallas_call x1, Pallas kernels, on_device(): pl.pallas_call(functools.partial(layer_kernel, (sections, experts, tensor...  54.9 us
    pallas_call x1, Pallas kernels, on_device(): pl.pallas_call(hand_over_kernel, out_shape=tuple((jax.ShapeDtypeStruct(pa...  1.4 us

profile of v2, /device:TPU:0, one launch (start us, length us, event | category | flops | bytes accessed | tf_op | source)
XLA Modules:
  0.0 57.0 jit_solution(4265487153753417297)
XLA Ops:
  0.6 54.9 %shard_map.94 = (bf16[8,1536]{1,0:T(8,128)(2,1)}, bf16[8,1536]{1,0:T(8,128)(2,1)}, f32[4,1536]{1,0:T(4,128)}) custom-call(bf16[8,1536]{1,0:T(8,128)(2,1)} %tokens_ref.1, s32[2,8]{1,0:T(2,128)} %bitcast.10, f32[4,6144]{1,0:T(4,128)} %bitcast.9, bf16[8,1536]{1,0:T(8,128)(2,1)} %grad_out_ref.1, bf16[6144,1024]{1,0:T(8,128)(2,1)} %bitcast.6, ...), custom_call_target="tpu_custom_call" | custom-call | tf_op jit(solution)/shard_map/pallas_call | solution.py:437
  55.6 1.4 %shard_map.95 = (bf16[8,1536]{1,0:T(8,128)(2,1)}, bf16[8,1536]{1,0:T(8,128)(2,1)}, f32[4,1536]{1,0:T(4,128)}) custom-call(bf16[8,1536]{1,0:T(8,128)(2,1)} %get-tuple-element.9.moe_ref, bf16[8,1536]{1,0:T(8,128)(2,1)} %get-tuple-element.10.tokens_ref, f32[4,1536]{1,0:T(4,128)} %get-tuple-element.11.router_ref), custom_call_target="tpu_custom_call" | custom-call | tf_op jit(solution)/shard_map/pallas_call | solution.py:479

commit v3 on v2

--- a/solution.py
+++ b/solution.py
@@ -197,7 +197,7 @@
     for k in near:
         hand_on(k)
 
-    tile = step_of(ff_dev, 256)
+    tile = step_of(ff_dev, 512)
     for j, q in enumerate(order):
         dy = j // 2
         if j == 1:
@@ -248,6 +248,8 @@
     weight_own[...] = jnp.broadcast_to(
         jnp.sum(jnp.where(is_own, weights, 0.0), axis=1, keepdims=True), (count, LANES)
     )
+
+    tile = step_of(ff_dev, 256)
 
     @pl.loop(0, ff_dev // tile)
     def _(n):
@@ -324,36 +326,14 @@
         first = pl.multiple_of(((section + ds) % sections) * experts * 16, 16)
         return pl.ds(first, experts * 16)
 
+    own_section = pl.multiple_of(section * experts * 16, 16)
+    spans = [slice(n * wide_tile, (n + 1) * wide_tile) for n in range(tiles)]
     to_plane = {}
-    for dy in outer[:-1]:
-        to_core[dy].wait_recv()
-        back(target_at(dy, False), dy * 2, dy)
-        for ds in range(sections):
-            k = ds * half + dy
-            to_plane[k] = remote(
-                partial.at[dy * 2, section_rows(ds), 0:quarter],
-                from_plane.at[k - 1],
-                plane_peer(k),
-            )
-
-    to_core[0].wait_recv()
-    spans = [slice(n * wide_tile, (n + 1) * wide_tile) for n in range(tiles)]
-    for n, cols in enumerate(spans):
-        back_tile(target_at(0, False), 0, 0, n)
-        for ds in range(1, sections):
-            k = ds * half
-            to_plane[k, n] = remote(
-                partial.at[0, section_rows(ds), cols],
-                from_plane.at[k - 1, :, cols],
-                plane_peer(k),
-            )
-
-    for k in far:
-        to_plane[k].wait_recv()
-    own_section = pl.multiple_of(section * experts * 16, 16)
     back_home = {}
-    for n, cols in enumerate(spans):
-        for k in near:
+
+    def finish(n):
+        cols = spans[n]
+        for k in range(1, plane):
             to_plane[k, n].wait_recv()
 
         @pl.loop(0, experts)
@@ -372,6 +352,23 @@
                 from_expert.at[k - 1, :, cols],
                 expert_peer(k),
             )
+
+    for n, cols in enumerate(spans):
+        for dy in outer:
+            if n == 0:
+                to_core[dy].wait_recv()
+            back_tile(target_at(dy, False), dy * 2, dy, n)
+            for ds in range(sections):
+                k = ds * half + dy
+                if k:
+                    to_plane[k, n] = remote(
+                        partial.at[dy * 2, section_rows(ds), cols],
+                        from_plane.at[k - 1, :, cols],
+                        plane_peer(k),
+                    )
+        if n:
+            finish(n - 1)
+    finish(tiles - 1)
 
     for copy in gw_over_expert:
         copy.wait_recv()
@@ -429,9 +426,7 @@
     groups = sections * experts
     count = groups * 8
     tiles = quarter // step_of(quarter, 512)
-    near = sections - 1
-    copies = (2 + tiles) * (experts - 1) + (1 + experts) * (plane - 1) + plane + half + 1
-    copies += plane - 1 - near + tiles * near
+    copies = (2 + tiles) * (experts - 1) + (1 + experts + tiles) * (plane - 1) + plane + half + 1
     vmem = pl.BlockSpec(memory_space=pltpu.VMEM)
     hbm = pl.BlockSpec(memory_space=pl.ANY)
     moe_out, grad_tokens, grad_router = pl.pallas_call(

time: 57.2 us -> 53.8 us (0.941)
  Pallas kernels: 56.3 us -> 53 us
    pallas_call x1, Pallas kernels: 54.9 us -> 51.6 us  [on_device(): pl.pallas_call(functools.partial(layer_kernel, (sections, experts, tensor...]
where the time goes in v3:
time: 53.8 us; the launch traced here: 53.6 us
  Pallas kernels  53 us (99%)
  between operations  0.64 us (1%)
    pallas_call x1, Pallas kernels, on_device(): pl.pallas_call(functools.partial(layer_kernel, (sections, experts, tensor...  51.6 us
    pallas_call x1, Pallas kernels, on_device(): pl.pallas_call(hand_over_kernel, out_shape=tuple((jax.ShapeDtypeStruct(pa...  1.4 us

profile of v3, /device:TPU:0, one launch (start us, length us, event | category | flops | bytes accessed | tf_op | source)
XLA Modules:
  0.0 53.6 jit_solution(15219664341985084137)
XLA Ops:
  0.6 51.6 %shard_map.94 = (bf16[8,1536]{1,0:T(8,128)(2,1)}, bf16[8,1536]{1,0:T(8,128)(2,1)}, f32[4,1536]{1,0:T(4,128)}) custom-call(bf16[8,1536]{1,0:T(8,128)(2,1)} %tokens_ref.1, s32[2,8]{1,0:T(2,128)} %bitcast.10, f32[4,6144]{1,0:T(4,128)} %bitcast.9, bf16[8,1536]{1,0:T(8,128)(2,1)} %grad_out_ref.1, bf16[6144,1024]{1,0:T(8,128)(2,1)} %bitcast.6, ...), custom_call_target="tpu_custom_call" | custom-call | tf_op jit(solution)/shard_map/pallas_call | solution.py:432
  52.2 1.4 %shard_map.95 = (bf16[8,1536]{1,0:T(8,128)(2,1)}, bf16[8,1536]{1,0:T(8,128)(2,1)}, f32[4,1536]{1,0:T(4,128)}) custom-call(bf16[8,1536]{1,0:T(8,128)(2,1)} %get-tuple-element.9.moe_ref, bf16[8,1536]{1,0:T(8,128)(2,1)} %get-tuple-element.10.tokens_ref, f32[4,1536]{1,0:T(4,128)} %get-tuple-element.11.router_ref), custom_call_target="tpu_custom_call" | custom-call | tf_op jit(solution)/shard_map/pallas_call | solution.py:474
